TPU v7x, 512 devices: a whole 4x8x8 slice. The times are simulated.
512 devices in a mesh: rep: 64 (over x, y, core), fsdp: 8 (over z).
Axes of the slice: x: 4, y: 8, z: 8, core: 2. Of those that a mesh axis runs over, the one named last changes fastest.
Arguments:
- base_weight: bfloat16 [32, 28672], P('fsdp'), may hold values from -6 to 6
- local_weight: bfloat16 [64, 32, 28672], P('rep', 'fsdp'), may hold values from -42 to 42
- momentum: float32 [32, 28672], P('fsdp'), may hold values from -3 to 3
Outputs:
- new_base: bfloat16 [32, 28672], replicated
- new_momentum: float32 [32, 28672], P('fsdp')
All inputs are finite; a program needn't handle non-finite values.
Results may differ from a plain program's by a relative error of at most 0.0027.
Values may be sent and summed in bfloat16 or wider, within the bound.
A program may use at most 128 MiB of HBM per device.

v0:
```python
import jax
import jax.numpy as jnp
from jax import lax
from jax.sharding import PartitionSpec as P


def spread_rows(mine):
    return lax.all_gather(mine, "fsdp", axis=0, tiled=True)


def shards(base_weight, local_weight, momentum):
    base_f = base_weight.astype(jnp.float32)
    delta = (base_f - local_weight[0].astype(jnp.float32)).astype(jnp.bfloat16)
    delta = lax.optimization_barrier(delta)
    replicas = lax.axis_size("rep")
    outer_grad = lax.psum(delta.astype(jnp.float32), "rep") / replicas
    new_momentum = 0.9 * momentum + outer_grad
    mine = (base_f - 0.7 * (outer_grad + 0.9 * new_momentum)).astype(jnp.bfloat16)
    new_base = spread_rows(mine)
    return (new_base, new_momentum)


def solution(mesh):
    return jax.shard_map(
        shards,
        mesh=mesh,
        in_specs=(P("fsdp", None), P("rep", "fsdp", None), P("fsdp", None)),
        out_specs=(P(), P("fsdp", None)),
        check_vma=False,
    )
```

profile of v0, /device:TPU:1, one launch (start us, length us, event | category | flops | bytes accessed | tf_op | source)
XLA Modules:
  0.0 312.3 jit_solution(2117048972762789391)
XLA Ops:
  7.2 0.0 all-gather.3.cloned.1.call-start
  7.2 1.2 fusion
  8.4 250.3 %all-reduce.1 = f32[4,28672]{1,0:T(4,128)S(1)} all-reduce(bf16[4,28672]{1,0:T(4,128)(2,1)S(1)} %fusion), channel_id=1, replica_groups=mesh['rep'=64,'fsdp'=8] {'rep'}, use_global_device_ids=true, to_apply=%region_0.0 | all-reduce | flops 114688 | bytes 688128 | tf_op jit(solution)/shard_map/psum | solution.py:16
  258.7 2.3 fusion.2
  261.0 0.0 all-gather.3.cloned.1.call-update
  261.0 41.8 %all-gather.3.cloned.1.call-done = bf16[8,4,28672]{2,1,0:T(4,128)(2,1)} async-done(((bf16[1,4,28672]{2,1,0:T(4,128)(2,1)}), bf16[8,4,28672]{2,1,0:T(4,128)(2,1)}) %all-gather.3.cloned.1.call-update) | async-done | bytes 1835024 | tf_op jit(solution)/shard_map/all_gather | solution.py:8
  302.8 2.6 reshape.8
Async XLA Ops:
  7.2 295.6 %all-gather.3.cloned.1.call-start = ((), (), s32[]{:S(2)}) async-start(), calls=%async_computation | async-start | bytes 2064384 | tf_op jit(solution)/shard_map/all_gather | solution.py:8
Sparse Core Ops, SparseCore 0:
  261.1 41.6 all-gather.2
where the time goes:
time: 316 us; the launch traced here: 312 us
  blocking collectives  250 us (79%)
  waiting for transfers between devices  41.8 us (13%)
  between operations  14 us (4%)
  other arithmetic  3.51 us (1%)
    psum x1, blocking collectives, shards(): outer_grad = lax.psum(delta.astype(jnp.float32), 'rep') / replicas  250 us
    all_gather x1, waiting for transfers between devices, spread_rows(): return lax.all_gather(mine, 'fsdp', axis=0, tiled=True)  41.8 us
  transfers between devices with their start and end apart: 1, of which 1 were waited for; matrix products, arithmetic and copies ran while one was open for 0% of the time, Pallas kernels for 0%

commit v1 on v0

v1 whole, which is shorter than its diff:
```python
import jax
import jax.numpy as jnp
from jax import lax
from jax.experimental import pallas as pl
from jax.experimental.pallas import tpu as pltpu
from jax.sharding import PartitionSpec as P

FF = 28672
NX, NY, NZ = 4, 8, 8
G = NX * 2
SEG = FF // G
PAIR = SEG // (NY // 2)
WIDE, SHIFT, NARROW = 512, 384, 384
f32, bf16 = jnp.float32, jnp.bfloat16


def kernel(base_h, local_h, mom_h, newb_h, newm_h, base_v, local_v, mom_v, send1, recv1, part, recv2, own_nb, zbuf,
           gath, nm, in_sem, out_sem, ssem, r1, r2, rz, ry_m, ry_b, rx_m, rx_b, rc_m, rc_b):
    rep = lax.axis_index("rep")
    z = lax.axis_index("fsdp")
    x = rep // (2 * NY)
    y = (rep // 2) % NY
    c = rep % 2
    g = x * 2 + c
    odd = y % 2

    def at(x_, y_, c_, z_):
        return {"rep": (x_ * NY + y_) * 2 + c_, "fsdp": z_}

    def g_peer(k):
        h = (g + k) % G
        return h, at(h // 2, y, h % 2, z)

    def y_peer(k):
        h = (y + k) % NY
        return h, at(x, h, c, z)

    def z_peer(k):
        h = (z + k) % NZ
        return h, at(x, y, c, h)

    barrier = pltpu.get_barrier_semaphore()
    for k in range(1, 8):
        for dev in (g_peer(k)[1], y_peer(k)[1], z_peer(k)[1]):
            pl.semaphore_signal(barrier, inc=1, device_id=dev, device_id_type=pl.DeviceIdType.MESH)

    def remote(src, dst, send, recv, dev):
        copy = pltpu.make_async_remote_copy(src_ref=src, dst_ref=dst, send_sem=send, recv_sem=recv, device_id=dev,
                                            device_id_type=pl.DeviceIdType.MESH)
        copy.start()

    def drain(ref, sem):
        pltpu.make_async_copy(ref, ref, sem).wait()

    def window(h, j):
        return pl.multiple_of(h * SEG + (j // 2) * PAIR + (j % 2) * SHIFT, 128)

    col = window(g, y)
    in_base = pltpu.make_async_copy(base_h, base_v, in_sem.at[0])
    in_local = pltpu.make_async_copy(local_h.at[0], local_v, in_sem.at[1])
    in_mom = pltpu.make_async_copy(mom_h.at[:, pl.ds(col, WIDE)], mom_v, in_sem.at[2])
    in_local.start()
    in_base.start()
    in_mom.start()
    in_local.wait()
    in_base.wait()

    for k in list(range(1, 8)) + [0]:
        h, dev = g_peer(k)
        cols = pl.ds(pl.multiple_of(h * SEG, 128), SEG)
        send1[k] = (base_v[:, cols].astype(f32) - local_v[:, cols].astype(f32)).astype(bf16)
        if k == 1:
            pl.semaphore_wait(barrier, 21)
        if k:
            remote(send1.at[k], recv1.at[k - 1], ssem.at[0], r1, dev)
    drain(recv1, r1)
    total = send1[0].astype(f32)
    for k in range(7):
        total += recv1[k].astype(f32)
    part[...] = total
    for k in range(1, 8):
        j, dev = y_peer(k)
        lo = pl.multiple_of((j // 2) * PAIR + (j % 2) * SHIFT, 128)
        remote(part.at[:, pl.ds(lo, WIDE)], recv2.at[k - 1], ssem.at[1], r2, dev)
    in_mom.wait()
    mine = pl.multiple_of((y // 2) * PAIR + odd * SHIFT, 128)
    total = part[:, pl.ds(mine, WIDE)]
    drain(recv2, r2)
    for k in range(7):
        total += recv2[k]
    grad = total * (1.0 / 64.0)
    new_m = 0.9 * mom_v[...] + grad
    b = base_v[:, pl.ds(col, WIDE)].astype(f32)
    new_b = (b - 0.7 * (grad + 0.9 * new_m)).astype(bf16)
    own_nb[...] = new_b
    for k in range(1, 8):
        _, dev = z_peer(k)
        remote(own_nb, zbuf.at[z], ssem.at[2], rz, dev)

    even_cols = pl.ds(col, WIDE)
    odd_cols = pl.ds(pl.multiple_of(col + 128, 128), NARROW)

    @pl.when(odd == 0)
    def _():
        nm[:, even_cols] = new_m
        for k in range(1, 8):
            remote(nm.at[:, even_cols], nm.at[:, even_cols], ssem.at[3], ry_m, y_peer(k)[1])

    @pl.when(odd == 1)
    def _():
        nm[:, odd_cols] = new_m[:, 128:]
        for k in range(1, 8):
            remote(nm.at[:, odd_cols], nm.at[:, odd_cols], ssem.at[3], ry_m, y_peer(k)[1])

    drain(zbuf.at[pl.ds(0, 7)], rz)
    zbuf[z] = new_b
    slab = jnp.concatenate([zbuf[i].astype(f32) for i in range(NZ)], axis=0).astype(bf16)

    @pl.when(odd == 0)
    def _():
        gath[:, even_cols] = slab
        for k in range(1, 8):
            remote(gath.at[:, even_cols], gath.at[:, even_cols], ssem.at[4], ry_b, y_peer(k)[1])

    @pl.when(odd == 1)
    def _():
        gath[:, odd_cols] = slab[:, 128:]
        for k in range(1, 8):
            remote(gath.at[:, odd_cols], gath.at[:, odd_cols], ssem.at[4], ry_b, y_peer(k)[1])

    n_even = SEG - WIDE
    n_odd = SEG - NARROW

    def drain_y(buf, sem):
        @pl.when(odd == 0)
        def _():
            drain(buf.at[:, pl.ds(0, n_even)], sem)

        @pl.when(odd == 1)
        def _():
            drain(buf.at[:, pl.ds(0, n_odd)], sem)

    def seg(buf, h):
        return buf.at[:, pl.ds(pl.multiple_of(h * SEG, 128), SEG)]

    partner = at(x, y, 1 - c, z)

    def spread(buf, sems, send):
        for k in (1, 3, 2):
            dev = at((x + k) % NX, y, c, z)
            remote(seg(buf, g), seg(buf, g), send, sems.at[k - 1], dev)

    drain_y(nm, ry_m)
    spread(nm, rx_m, ssem.at[5])
    remote(seg(nm, g), seg(nm, g), ssem.at[6], rc_m.at[0], partner)
    drain_y(gath, ry_b)
    spread(gath, rx_b, ssem.at[7])
    remote(seg(gath, g), seg(gath, g), ssem.at[8], rc_b.at[0], partner)

    for buf, rx, rc, send in ((nm, rx_m, rc_m, ssem.at[6]), (gath, rx_b, rc_b, ssem.at[8])):
        for k in (1, 3, 2):
            h = ((x - k) % NX) * 2 + c
            drain(seg(buf, h), rx.at[k - 1])
            remote(seg(buf, h), seg(buf, h), send, rc.at[k], partner)
    for buf, rc in ((nm, rc_m), (gath, rc_b)):
        for k in range(4):
            drain(seg(buf, 0), rc.at[k])
    out_m = pltpu.make_async_copy(nm, newm_h, out_sem.at[0])
    out_b = pltpu.make_async_copy(gath, newb_h, out_sem.at[1])
    out_m.start()
    out_b.start()
    drain(recv1, ssem.at[0])
    drain(recv2, ssem.at[1])
    drain(zbuf.at[pl.ds(0, 7)], ssem.at[2])

    @pl.when(odd == 0)
    def _():
        drain(nm.at[:, pl.ds(0, 7 * WIDE)], ssem.at[3])
        drain(gath.at[:, pl.ds(0, 7 * WIDE)], ssem.at[4])

    @pl.when(odd == 1)
    def _():
        drain(nm.at[:, pl.ds(0, 7 * NARROW)], ssem.at[3])
        drain(gath.at[:, pl.ds(0, 7 * NARROW)], ssem.at[4])

    drain(nm.at[:, pl.ds(0, 3 * SEG)], ssem.at[5])
    drain(nm.at[:, pl.ds(0, 4 * SEG)], ssem.at[6])
    drain(gath.at[:, pl.ds(0, 3 * SEG)], ssem.at[7])
    drain(gath.at[:, pl.ds(0, 4 * SEG)], ssem.at[8])
    out_m.wait()
    out_b.wait()


def shards(base_weight, local_weight, momentum):
    any_ = pl.BlockSpec(memory_space=pl.ANY)
    dma = pltpu.SemaphoreType.DMA
    return pl.pallas_call(
        kernel,
        out_shape=(jax.ShapeDtypeStruct((32, FF), bf16), jax.ShapeDtypeStruct((4, FF), f32)),
        in_specs=[any_] * 3,
        out_specs=(any_, any_),
        scratch_shapes=[
            pltpu.VMEM((4, FF), bf16),
            pltpu.VMEM((4, FF), bf16),
            pltpu.VMEM((4, WIDE), f32),
            pltpu.VMEM((8, 4, SEG), bf16),
            pltpu.VMEM((7, 4, SEG), bf16),
            pltpu.VMEM((4, SEG), f32),
            pltpu.VMEM((7, 4, WIDE), f32),
            pltpu.VMEM((4, WIDE), bf16),
            pltpu.VMEM((8, 4, WIDE), bf16),
            pltpu.VMEM((32, FF), bf16),
            pltpu.VMEM((4, FF), f32),
            dma((3,)),
            dma((2,)),
            dma((9,)),
            dma, dma, dma, dma, dma,
            dma((3,)), dma((3,)), dma((4,)), dma((4,)),
        ],
        compiler_params=pltpu.CompilerParams(collective_id=0, has_side_effects=True, vmem_limit_bytes=32 * 2**20),
        cost_estimate=pl.CostEstimate(flops=4 * FF * 8, bytes_accessed=32 * FF * 4, transcendentals=0),
    )(base_weight, local_weight, momentum)


def solution(mesh):
    return jax.shard_map(
        shards,
        mesh=mesh,
        in_specs=(P("fsdp", None), P("rep", "fsdp", None), P("fsdp", None)),
        out_specs=(P(), P("fsdp", None)),
        check_vma=False,
    )
```

time: 316 us -> 55 us (0.17)
  the two profiles are of different devices: /device:TPU:1 before, /device:TPU:7 now
where the time goes in v1:
time: 55 us; the launch traced here: 54.8 us
  Pallas kernels  49.3 us (90%)
  local copies, waits for them, and re-layouts  4.89 us (9%)
  between operations  0.65 us (1%)
    pallas_call x1, Pallas kernels, shards(): pl.pallas_call(kernel, out_shape=(jax.ShapeDtypeStruct((32, FF), bf16), j...  49.3 us
    unnamed x8, local copies, waits for them, and re-layouts  4.89 us

profile of v1, /device:TPU:7, one launch (start us, length us, event | category | flops | bytes accessed | tf_op | source)
XLA Modules:
  0.0 54.8 jit_solution(6429949243920900443)
XLA Ops:
  0.6 0.0 copy-start
  0.6 1.0 %copy-done = f32[4,28672]{1,0:T(4,128)S(1)} copy-done((f32[4,28672]{1,0:T(4,128)S(1)}, f32[4,28672]{1,0:T(4,128)}, u32[]{:S(2)}) %copy-start) | copy-done | bytes 458776
  1.6 0.0 copy-start.1
  1.7 0.9 %copy-done.1 = bf16[4,28672]{1,0:T(4,128)(2,1)S(1)} copy-done((bf16[4,28672]{1,0:T(4,128)(2,1)S(1)}, bf16[4,28672]{1,0:T(4,128)(2,1)}, u32[]{:S(2)}) %copy-start.1) | copy-done | bytes 229400
  2.6 0.0 copy-start.2
  2.6 0.9 %copy-done.2 = bf16[1,4,28672]{2,1,0:T(4,128)(2,1)S(1)} copy-done((bf16[1,4,28672]{2,1,0:T(4,128)(2,1)S(1)}, bf16[1,4,28672]{2,1,0:T(4,128)(2,1)}, u32[]{:S(2)}) %copy-start.2) | copy-done | bytes 229400
  3.5 49.3 %shard_map.50 = (bf16[32,28672]{1,0:T(8,128)(2,1)S(1)}, f32[4,28672]{1,0:T(4,128)S(1)}) custom-call(bf16[4,28672]{1,0:T(4,128)(2,1)S(1)} %copy-done.1, bf16[1,4,28672]{2,1,0:T(4,128)(2,1)S(1)} %copy-done.2, f32[4,28672]{1,0:T(4,128)S(1)} %copy-done), custom_call_target="tpu_custom_call" | custom-call | flops 917504 | bytes 3670016 | tf_op jit(solution)/shard_map/pallas_call | solution.py:197
  52.8 1.2 %copy.7 = bf16[32,28672]{1,0:T(8,128)(2,1)} copy(bf16[32,28672]{1,0:T(8,128)(2,1)S(1)} %get-tuple-element.4) | data formatting | bytes 3670016
  54.0 0.8 %copy.8 = f32[4,28672]{1,0:T(4,128)} copy(f32[4,28672]{1,0:T(4,128)S(1)} %get-tuple-element.5) | data formatting | bytes 917504
Async XLA Ops:
  0.6 1.0 %copy-start = (f32[4,28672]{1,0:T(4,128)S(1)}, f32[4,28672]{1,0:T(4,128)}, u32[]{:S(2)}) copy-start(f32[4,28672]{1,0:T(4,128)} %mom_h.1) | copy-start | bytes 1376260
  1.6 0.9 %copy-start.1 = (bf16[4,28672]{1,0:T(4,128)(2,1)S(1)}, bf16[4,28672]{1,0:T(4,128)(2,1)}, u32[]{:S(2)}) copy-start(bf16[4,28672]{1,0:T(4,128)(2,1)} %base_h.1) | copy-start | bytes 688132
  2.6 0.9 %copy-start.2 = (bf16[1,4,28672]{2,1,0:T(4,128)(2,1)S(1)}, bf16[1,4,28672]{2,1,0:T(4,128)(2,1)}, u32[]{:S(2)}) copy-start(bf16[1,4,28672]{2,1,0:T(4,128)(2,1)} %local_h.1) | copy-start | bytes 688132

commit v2 on v0

v2 whole, which is shorter than its diff:
```python
import jax
import jax.numpy as jnp
from jax import lax
from jax.experimental import pallas as pl
from jax.experimental.pallas import tpu as pltpu
from jax.sharding import PartitionSpec as P

FF = 28672
NX, NY, NZ = 4, 8, 8
G = NX * 2
BLOCK = FF // NY
CHIP = BLOCK // NX
WIDE, NARROW = 512, 384
SUM_SLOTS = (4, 3, -3, 2, -2, 1, -1, 0)
SLOTS = (0, 1, -1, 2, -2, 3, -3, 4)
GROUPS = ((0, 1), (1, 2), (3, 2), (5, 3))
f32, bf16 = jnp.float32, jnp.bfloat16
MESH = pl.DeviceIdType.MESH


def slot_of(offset):
    return SLOTS.index((offset + 3) % NY - 3)


def place():
    rep = lax.axis_index("rep")
    return rep // (2 * NY), (rep // 2) % NY, rep % 2, lax.axis_index("fsdp")


def kernel(base_h, local_h, mom_h, gath, gath_m, base_v, local_v, mom_v, send1, recv1, part, recv2, own_nb, zbuf,
           in_sem, s1, s2, sz, sy_m, sy_b, sx_m, sx_b, sc_m, sc_b, r1, r2, rz, ry_m, ry_b, rx_m, rx_b, rh_b, rc_m, rc_b):
    x, y, c, z = place()

    def at(x_, y_, c_, z_):
        return {"rep": (x_ * NY + y_) * 2 + c_, "fsdp": z_}

    def g_peer(k):
        h = (x * 2 + c + k) % G
        return h // 2, h % 2

    def y_peer(k):
        return at(x, (y + k) % NY, c, z)

    def x_peer(k):
        return at((x + k) % NX, y, c, z)

    partner = at(x, y, 1 - c, z)
    barrier = pltpu.get_barrier_semaphore()
    for k in range(1, 8):
        gx, gc = g_peer(k)
        for dev in (at(gx, y, gc, z), y_peer(k), at(x, y, c, (z + k) % NZ)):
            pl.semaphore_signal(barrier, inc=1, device_id=dev, device_id_type=MESH)

    def remote(src, dst, send, recv, dev):
        pltpu.make_async_remote_copy(src_ref=src, dst_ref=dst, send_sem=send, recv_sem=recv, device_id=dev,
                                     device_id_type=MESH).start()

    def drain(ref, sem):
        pltpu.make_async_copy(ref, ref, sem).wait()

    def window(j, x_, c_):
        return pl.ds(pl.multiple_of(j * BLOCK + x_ * CHIP + c_ * NARROW, 128), WIDE)

    mine = window(y, x, c)
    in_local = pltpu.make_async_copy(local_h.at[0], local_v, in_sem.at[0])
    in_base = pltpu.make_async_copy(base_h, base_v, in_sem.at[1])
    in_mom = pltpu.make_async_copy(mom_h.at[:, mine], mom_v, in_sem.at[2])
    in_local.start()
    in_base.start()
    in_mom.start()
    in_local.wait()
    in_base.wait()

    for half in range(2):
        for k in list(range(1, 8)) + [0]:
            gx, gc = g_peer(k)
            for i in range(4):
                cols = window((y + SUM_SLOTS[half * 4 + i]) % NY, gx, gc)
                send1[half, k, i] = (base_v[:, cols].astype(f32) - local_v[:, cols].astype(f32)).astype(bf16)
            if half == 0 and k == 1:
                pl.semaphore_wait(barrier, 21)
            if k:
                remote(send1.at[half, k], recv1.at[half, k - 1], s1, r1.at[half], at(gx, y, gc, z))
    for half in range(2):
        drain(recv1.at[half], r1.at[half])
        for i in range(4):
            total = send1[half, 0, i].astype(f32)
            for k in range(7):
                total += recv1[half, k, i].astype(f32)
            part[half * 4 + i] = total
            off = SUM_SLOTS[half * 4 + i]
            if off:
                remote(part.at[half * 4 + i], recv2.at[(off - 1) % NY], s2, r2, y_peer(off))
    total = part[7]
    in_mom.wait()
    b = base_v[:, mine].astype(f32)
    drain(recv2, r2)
    for k in range(7):
        total += recv2[k]
    grad = total * (1.0 / 64.0)
    new_m = 0.9 * mom_v[...] + grad
    new_b = (b - 0.7 * (grad + 0.9 * new_m)).astype(bf16)
    own_nb[...] = new_b
    for k in range(1, 8):
        remote(own_nb, zbuf.at[z], sz, rz, at(x, y, c, (z + k) % NZ))
    zbuf[z] = new_b

    def gather(par):
        lo, w = (0, WIDE) if par == 0 else (128, NARROW)
        other = WIDE + NARROW - w

        def cols_of(x_):
            return pl.ds(pl.multiple_of(x_ * CHIP + par * WIDE, 128), w)

        own = cols_of(x)

        def blocks(buf, g, x_):
            return buf.at[pl.ds(*g), :, cols_of(x_)]

        def pass_on(buf, g, x_, send, recv):
            remote(blocks(buf, g, x_), blocks(buf, g, x_), send, recv, partner)

        gath_m[0, :, own] = new_m[:, lo:]
        for k in SLOTS[1:]:
            remote(gath_m.at[0, :, own], gath_m.at[slot_of(-k), :, own], sy_m, ry_m, y_peer(k))
        drain(zbuf.at[pl.ds(0, 7)], rz)
        slab = jnp.concatenate([zbuf[i][:, lo:].astype(f32) for i in range(NZ)], axis=0).astype(bf16)
        gath[0, :, own] = slab
        for k in SLOTS[1:]:
            slot = slot_of(-k)
            group = (slot + 1) // 2 if slot < 7 else 3
            remote(gath.at[0, :, own], gath.at[slot, :, own], sy_b, ry_b.at[group - 1], y_peer(k))
        every = (0, NY)

        def feed(i):
            g = GROUPS[i]
            if i:
                drain(blocks(gath, g, 0), ry_b.at[i - 1])
            for d, k in enumerate((1, -1)):
                remote(blocks(gath, g, x), blocks(gath, g, x), sx_b, rx_b.at[d, i], x_peer(k))
            pass_on(gath, g, x, sc_b, rc_b.at[0, i])

        def half_of(i, d, x_):
            return gath.at[pl.ds(*GROUPS[i]), pl.ds(d * 16, 16), cols_of(x_)]

        def take(i):
            for d, k in enumerate((1, -1)):
                from_ = (x - k) % NX
                drain(blocks(gath, GROUPS[i], 0), rx_b.at[d, i])
                remote(half_of(i, d, from_), half_of(i, d, from_), sx_b, rh_b.at[d, i], x_peer(k))
                pass_on(gath, GROUPS[i], from_, sc_b, rc_b.at[1 + d, i])

        feed(0)
        drain(gath_m.at[pl.ds(0, 7), :, cols_of(0)], ry_m)
        for k in (1, 3, 2):
            remote(blocks(gath_m, every, x), blocks(gath_m, every, x), sx_m, rx_m.at[k - 1], x_peer(k))
        pass_on(gath_m, every, x, sc_m, rc_m.at[0])
        feed(1)
        take(0)
        feed(2)
        for k in (1, 3, 2):
            drain(blocks(gath_m, every, 0), rx_m.at[k - 1])
            pass_on(gath_m, every, (x - k) % NX, sc_m, rc_m.at[k])
        take(1)
        feed(3)
        take(2)
        take(3)
        for i in range(4):
            for d in range(2):
                drain(half_of(i, d, 0), rh_b.at[d, i])
            pass_on(gath, GROUPS[i], (x + 2) % NX, sc_b, rc_b.at[3, i])
        drain(gath_m.at[pl.ds(0, 7), :, cols_of(0)], sy_m)
        drain(gath.at[pl.ds(0, 7), :, cols_of(0)], sy_b)
        drain(gath_m.at[:, :, pl.ds(0, 3 * w)], sx_m)
        drain(gath.at[:, :, pl.ds(0, 3 * w)], sx_b)
        drain(gath_m.at[:, :, pl.ds(0, 4 * w)], sc_m)
        drain(gath.at[:, :, pl.ds(0, 4 * w)], sc_b)
        for k in range(4):
            drain(gath_m.at[:, :, pl.ds(0, other)], rc_m.at[k])
            for i in range(4):
                drain(gath.at[pl.ds(*GROUPS[i]), :, pl.ds(0, other)], rc_b.at[k, i])

    for par in range(2):
        pl.when(c == par)(lambda par=par: gather(par))
    drain(recv1, s1)
    drain(recv2, s2)
    drain(zbuf.at[pl.ds(0, 7)], sz)


def flush_kernel(gath, gath_m, newb, newm, sem):
    y = place()[1]
    copies = []
    for s, off in enumerate(SLOTS):
        cols = pl.ds(pl.multiple_of((y + off) % NY * BLOCK, 128), BLOCK)
        copies.append(pltpu.make_async_copy(gath.at[s], newb.at[:, cols], sem.at[0, s]))
        copies.append(pltpu.make_async_copy(gath_m.at[s], newm.at[:, cols], sem.at[1, s]))
    for copy in copies:
        copy.start()
    for copy in copies:
        copy.wait()


def shards(base_weight, local_weight, momentum):
    hbm, vmem = pl.BlockSpec(memory_space=pltpu.HBM), pl.BlockSpec(memory_space=pltpu.VMEM)
    dma = pltpu.SemaphoreType.DMA
    gath, gath_m = pl.pallas_call(
        kernel,
        out_shape=(pltpu.VMEM((NY, 32, BLOCK), bf16), pltpu.VMEM((NY, 4, BLOCK), f32)),
        in_specs=[hbm] * 3,
        out_specs=(vmem, vmem),
        scratch_shapes=[
            pltpu.VMEM((4, FF), bf16),
            pltpu.VMEM((4, FF), bf16),
            pltpu.VMEM((4, WIDE), f32),
            pltpu.VMEM((2, 8, 4, 4, WIDE), bf16),
            pltpu.VMEM((2, 7, 4, 4, WIDE), bf16),
            pltpu.VMEM((8, 4, WIDE), f32),
            pltpu.VMEM((7, 4, WIDE), f32),
            pltpu.VMEM((4, WIDE), bf16),
            pltpu.VMEM((8, 4, WIDE), bf16),
            dma((3,)),
            dma, dma, dma, dma, dma, dma, dma, dma, dma,
            dma((2,)), dma, dma, dma, dma((3,)), dma((3,)), dma((2, 4)), dma((2, 4)), dma((4,)), dma((4, 4)),
        ],
        compiler_params=pltpu.CompilerParams(collective_id=0, has_side_effects=True, vmem_limit_bytes=32 * 2**20),
        cost_estimate=pl.CostEstimate(flops=4 * FF * 8, bytes_accessed=32 * FF * 4, transcendentals=0),
    )(*(pltpu.with_memory_space_constraint(a, pltpu.HBM) for a in (base_weight, local_weight, momentum)))
    return pl.pallas_call(
        flush_kernel,
        out_shape=(pltpu.HBM((32, FF), bf16), pltpu.HBM((4, FF), f32)),
        in_specs=[vmem, vmem],
        out_specs=(hbm, hbm),
        scratch_shapes=[dma((2, NY))],
        cost_estimate=pl.CostEstimate(flops=0, bytes_accessed=32 * FF * 4, transcendentals=0),
    )(*(pltpu.with_memory_space_constraint(a, pltpu.VMEM) for a in (gath, gath_m)))


def solution(mesh):
    return jax.shard_map(
        shards,
        mesh=mesh,
        in_specs=(P("fsdp", None), P("rep", "fsdp", None), P("fsdp", None)),
        out_specs=(P(), P("fsdp", None)),
        check_vma=False,
    )
```

time: 316 us -> 47.4 us (0.15); the launches traced: 312 us -> 47.3 us
  blocking collectives: 250 us -> 0 us
  Pallas kernels: 0 us -> 46.6 us
  waiting for transfers between devices: 41.8 us -> 0 us
  between operations: 14 us -> 0.64 us
  other arithmetic: 3.51 us -> 0 us
    psum x1 -> x0, blocking collectives: 250 us -> none  [shards(): outer_grad = lax.psum(delta.astype(jnp.float32), 'rep') / replicas]
    pallas_call x0 -> x2, Pallas kernels: none -> 46.6 us  [the longest x1 45.1 us: shards(): pl.pallas_call(kernel, out_shape=(pltpu.VMEM((NY, 32, BLOCK), bf16), pltp...]
    all_gather x1 -> x0, waiting for transfers between devices: 41.8 us -> none  [spread_rows(): return lax.all_gather(mine, 'fsdp', axis=0, tiled=True)]
  transfers between devices with their start and end apart: 1 -> 0, of which waited for: 1 -> 0; matrix products, arithmetic and copies ran while one was open for 0% -> 0% of each run, Pallas kernels for 0% -> 0%
where the time goes in v2:
time: 47.4 us; the launch traced here: 47.3 us
  Pallas kernels  46.6 us (98%)
  between operations  0.64 us (1%)
    pallas_call x1, Pallas kernels, shards(): pl.pallas_call(kernel, out_shape=(pltpu.VMEM((NY, 32, BLOCK), bf16), pltp...  45.1 us
    pallas_call x1, Pallas kernels, shards(): pl.pallas_call(flush_kernel, out_shape=(pltpu.HBM((32, FF), bf16), pltpu....  1.52 us

profile of v2, /device:TPU:1, one launch (start us, length us, event | category | flops | bytes accessed | tf_op | source)
XLA Modules:
  0.0 47.3 jit_solution(15065239651299228069)
XLA Ops:
  0.6 45.1 %shard_map.50 = (bf16[8,32,3584]{2,1,0:T(8,128)(2,1)S(1)}, f32[8,4,3584]{2,1,0:T(4,128)S(1)}) custom-call(bf16[4,28672]{1,0:T(4,128)(2,1)} %base_h.1, bf16[1,4,28672]{2,1,0:T(4,128)(2,1)} %local_h.1, f32[4,28672]{1,0:T(4,128)} %mom_h.1), custom_call_target="tpu_custom_call" | custom-call | flops 917504 | bytes 3670016 | tf_op jit(solution)/shard_map/pallas_call | solution.py:206
  45.8 1.5 %shard_map.51 = (bf16[32,28672]{1,0:T(8,128)(2,1)}, f32[4,28672]{1,0:T(4,128)}) custom-call(bf16[8,32,3584]{2,1,0:T(8,128)(2,1)S(1)} %get-tuple-element.4.gath, f32[8,4,3584]{2,1,0:T(4,128)S(1)} %get-tuple-element.5.gath_m), custom_call_target="tpu_custom_call" | custom-call | bytes 3670016 | tf_op jit(solution)/shard_map/pallas_call | solution.py:228

commit v3 on v2

v3 whole, which is shorter than its diff:
```python
import jax
import jax.numpy as jnp
from jax import lax
from jax.experimental import pallas as pl
from jax.experimental.pallas import tpu as pltpu
from jax.sharding import PartitionSpec as P

FF = 28672
NX, NY, NZ = 4, 8, 8
BLOCK = FF // NY
CHIP = BLOCK // NX
WIDE, NARROW = 512, 384
SLOTS = (0, 1, -1, 2, -2, 3, -3, 4)
GROUPS = ((0, 0, 1), (0, 1, 4), (0, 5, 3), (1, 0, 4), (1, 4, 4))
DIRECT = (3, 4)
PLANE = sorted(((i, j, k) for i in range(NX) for j in range(NY) for k in range(2)),
               key=lambda d: (-min(d[0], NX - d[0]) - min(d[1], NY - d[1]), -d[2]))
f32, bf16 = jnp.float32, jnp.bfloat16
MESH = pl.DeviceIdType.MESH


def slot_of(offset):
    return SLOTS.index((offset + 3) % NY - 3)


def place():
    rep = lax.axis_index("rep")
    return rep // (2 * NY), (rep // 2) % NY, rep % 2, lax.axis_index("fsdp")


def kernel(base_h, local_h, mom_h, gath, gath_m, base_v, local_v, mom_v, send1, recv1, own_a, own_c, abuf, bbuf,
           cbuf, in_sem, send_sem, r1, rz_a, ry_a, ry_b, rz_b, rx_c, rz_c, ry_c, ry_m, rx_m, rx, rh, rf, rc, rc_c, rc_m):
    x, y, c, z = place()
    s1, sz_a, sy_a, sy_b, sz_b, sx_c, sz_c, sy_c, sy_m, sx_m, sx, sc, sc_m = (send_sem.at[i] for i in range(13))

    def at(x_, y_, c_, z_):
        return {"rep": (x_ * NY + y_) * 2 + c_, "fsdp": z_}

    def y_peer(k):
        return at(x, (y + k) % NY, c, z)

    def z_peer(k):
        return at(x, y, c, (z + k) % NZ)

    def x_peer(k):
        return at((x + k) % NX, y, c, z)

    partner = at(x, y, 1 - c, z)
    barrier = pltpu.get_barrier_semaphore()
    for dx, dy, dc in PLANE[:-1]:
        dev = at((x + dx) % NX, (y + dy) % NY, (c + dc) % 2, z)
        pl.semaphore_signal(barrier, inc=1, device_id=dev, device_id_type=MESH)
    for k in range(1, NZ):
        pl.semaphore_signal(barrier, inc=1, device_id=z_peer(k), device_id_type=MESH)

    def remote(src, dst, send, recv, dev):
        pltpu.make_async_remote_copy(src_ref=src, dst_ref=dst, send_sem=send, recv_sem=recv, device_id=dev,
                                     device_id_type=MESH).start()

    def drain(ref, sem):
        pltpu.make_async_copy(ref, ref, sem).wait()

    def window(j, x_, c_):
        return pl.ds(pl.multiple_of(j * BLOCK + x_ * CHIP + c_ * NARROW, 128), WIDE)

    mine = window(y, x, c)
    in_local = pltpu.make_async_copy(local_h.at[0], local_v, in_sem.at[0])
    in_base = pltpu.make_async_copy(base_h, base_v, in_sem.at[1])
    in_mom = pltpu.make_async_copy(mom_h.at[:, mine], mom_v, in_sem.at[2])
    in_local.start()
    in_base.start()
    in_mom.start()
    in_local.wait()
    in_base.wait()

    for k, (dx, dy, dc) in enumerate(PLANE):
        dev = (x + dx) % NX, (y + dy) % NY, (c + dc) % 2
        cols = window(dev[1], dev[0], dev[2])
        send1[k] = (base_v[:, cols].astype(f32) - local_v[:, cols].astype(f32)).astype(bf16)
        if k == 0:
            pl.semaphore_wait(barrier, len(PLANE) - 1 + NZ - 1)
        if k < 63:
            remote(send1.at[k], recv1.at[k], s1, r1.at[k // 32], at(*dev, z))
    total = send1[63].astype(f32)
    in_mom.wait()
    b = base_v[:, mine].astype(f32)
    for part in (range(32), range(32, 63)):
        drain(recv1.at[pl.ds(0, len(part))], r1.at[part[0] // 32])
        for k in part:
            total += recv1[k].astype(f32)
    grad = total * (1.0 / 64.0)
    new_m = 0.9 * mom_v[...] + grad
    new_b = (b - 0.7 * (grad + 0.9 * new_m)).astype(bf16)
    own_a[...] = new_b[:, :256]
    own_c[...] = new_b[:, 384:]
    abuf[z] = new_b[:, :256]
    bbuf[z, 0] = new_b[:, 256:384]
    cbuf[z, x] = new_b[:, 384:]
    for k in (2, 1, 3):
        remote(own_c, cbuf.at[z, x], sx_c, rx_c, x_peer(k))
    for k in SLOTS[:0:-1]:
        remote(own_a, abuf.at[z], sz_a, rz_a, z_peer(k))
        remote(bbuf.at[z, 0], bbuf.at[z, slot_of(-k)], sy_b, ry_b, y_peer(k))

    def rows(parts):
        return jnp.concatenate([p.astype(f32) for p in parts], axis=0).astype(bf16)

    def gather(par):
        lo, w = (0, WIDE) if par == 0 else (128, NARROW)
        other = WIDE + NARROW - w
        w_a = 256 - lo
        own = pl.ds(par * WIDE, w)
        cols = (pl.ds(par * WIDE, w_a), pl.ds(par * WIDE + w_a, 128), pl.ds(par * WIDE + w_a + 128, 128))

        def blocks(i, x_):
            part_, start, n = GROUPS[i]
            return gath.at[pl.ds(start, n), x_, :, cols[part_]]

        def halves(i, d, x_):
            part_, start, n = GROUPS[i]
            return gath.at[pl.ds(start, n), x_, pl.ds(d * 16, 16), cols[part_]]

        def pass_on(i, x_, k):
            remote(blocks(i, x_), blocks(i, x_), sc, rc.at[k, i], partner)

        def feed(i):
            if i in DIRECT:
                remote(blocks(i, x), blocks(i, x), sx, rf.at[i], x_peer(2))
            for d, k in enumerate((1, -1)):
                remote(blocks(i, x), blocks(i, x), sx, rx.at[d, i], x_peer(k))
            pass_on(i, x, 0)

        def take(i):
            for d, k in enumerate((1, -1)):
                from_ = (x - k) % NX
                drain(blocks(i, 0), rx.at[d, i])
                if i not in DIRECT:
                    remote(halves(i, d, from_), halves(i, d, from_), sx, rh.at[d, i], x_peer(k))
                pass_on(i, from_, 1 + d)

        def far(i):
            if i in DIRECT:
                drain(blocks(i, 0), rf.at[i])
            else:
                for d in range(2):
                    drain(halves(i, d, 0), rh.at[d, i])
            pass_on(i, (x + 2) % NX, 3)

        def momentum(x_):
            return gath_m.at[:, x_, :, own]

        gath_m[0, x, :, own] = new_m[:, lo:]
        for k in SLOTS[:0:-1]:
            remote(gath_m.at[0, x, :, own], gath_m.at[slot_of(-k), x, :, own], sy_m, ry_m, y_peer(k))
        drain(cbuf.at[0, pl.ds(0, 3)], rx_c)
        for k in SLOTS[:0:-1]:
            remote(cbuf.at[z], cbuf.at[z], sz_c, rz_c, z_peer(k))
        drain(abuf.at[pl.ds(0, 7)], rz_a)
        gath[0, x, :, cols[0]] = rows([abuf[i][:, lo:] for i in range(NZ)])
        for k in SLOTS[1:]:
            slot = slot_of(-k)
            remote(gath.at[0, x, :, cols[0]], gath.at[slot, x, :, cols[0]], sy_a, ry_a.at[int(slot > 4)], y_peer(k))
        drain(bbuf.at[0, pl.ds(0, 7)], ry_b)
        for k in SLOTS[:0:-1]:
            remote(bbuf.at[z], bbuf.at[z], sz_b, rz_b, z_peer(k))
        feed(0)
        drain(gath_m.at[pl.ds(0, 7), 0, :, own], ry_m)
        for k in (2, 1, 3):
            remote(momentum(x), momentum(x), sx_m, rx_m.at[k - 1], x_peer(k))
        remote(momentum(x), momentum(x), sc_m, rc_m.at[0], partner)
        drain(cbuf.at[pl.ds(0, 7)], rz_c)
        for i in range(NX):
            gath[0, i, :, cols[2]] = rows([cbuf[j, i] for j in range(NZ)])
        for k in SLOTS[:0:-1]:
            slot = slot_of(-k)
            remote(gath.at[0, :, :, cols[2]], gath.at[slot, :, :, cols[2]], sy_c, ry_c.at[int(slot > 4)], y_peer(k))
        remote(gath.at[0, :, :, cols[2]], gath.at[0, :, :, cols[2]], sc, rc_c.at[0], partner)
        drain(blocks(1, 0), ry_a.at[0])
        feed(1)
        take(0)
        drain(blocks(2, 0), ry_a.at[1])
        feed(2)
        drain(bbuf.at[pl.ds(0, 7)], rz_b)
        for s in range(NY):
            gath[s, x, :, cols[1]] = rows([bbuf[i, s] for i in range(NZ)])
            if s == 3:
                feed(3)
        feed(4)
        take(1)
        for k in (1, 3, 2):
            drain(momentum(0), rx_m.at[k - 1])
            remote(momentum((x - k) % NX), momentum((x - k) % NX), sc_m, rc_m.at[k], partner)
        far(0)
        take(2)
        take(3)
        take(4)
        for i, near in ((1, pl.ds(1, 4)), (2, pl.ds(5, 3))):
            far(i)
            block = gath.at[near, :, :, cols[2]]
            drain(block, ry_c.at[i - 1])
            remote(block, block, sc, rc_c.at[i], partner)
        far(3)
        far(4)
        drain(gath_m.at[pl.ds(0, 7), 0, :, own], sy_m)
        drain(gath.at[pl.ds(0, 7), 0, :, cols[0]], sy_a)
        drain(gath.at[pl.ds(0, 7), :, :, cols[2]], sy_c)
        drain(gath_m.at[:, pl.ds(0, 3), :, own], sx_m)
        drain(gath_m.at[:, :, :, own], sc_m)
        drain(gath.at[:, pl.ds(0, 3), :, pl.ds(0, w_a + 128)], sx)
        drain(gath.at[:, :, :, own], sc)
        for k in range(4):
            drain(gath_m.at[:, 0, :, pl.ds(0, other)], rc_m.at[k])
            for i, (part_, start, n) in enumerate(GROUPS):
                drain(gath.at[pl.ds(start, n), 0, :, pl.ds(0, 128 if part_ else other - 256)], rc.at[k, i])
        for i, n in enumerate((1, 4, 3)):
            drain(gath.at[pl.ds(0, n), :, :, pl.ds(0, 128)], rc_c.at[i])

    for par in range(2):
        pl.when(c == par)(lambda par=par: gather(par))
    drain(recv1, s1)
    drain(abuf.at[pl.ds(0, 7)], sz_a)
    drain(bbuf.at[0, pl.ds(0, 7)], sy_b)
    drain(bbuf.at[pl.ds(0, 7)], sz_b)
    drain(cbuf.at[0, pl.ds(0, 3)], sx_c)
    drain(cbuf.at[pl.ds(0, 7)], sz_c)


def flush_kernel(gath, gath_m, newb, newm, sem):
    y = place()[1]
    copies = []
    for s, off in enumerate(SLOTS):
        for i in range(NX):
            cols = pl.ds(pl.multiple_of((y + off) % NY * BLOCK + i * CHIP, 128), CHIP)
            copies.append(pltpu.make_async_copy(gath.at[s, i], newb.at[:, cols], sem.at[0, s, i]))
            copies.append(pltpu.make_async_copy(gath_m.at[s, i], newm.at[:, cols], sem.at[1, s, i]))
    for copy in copies:
        copy.start()
    for copy in copies:
        copy.wait()


def shards(base_weight, local_weight, momentum):
    hbm, vmem = pl.BlockSpec(memory_space=pltpu.HBM), pl.BlockSpec(memory_space=pltpu.VMEM)
    dma = pltpu.SemaphoreType.DMA
    gath, gath_m = pl.pallas_call(
        kernel,
        out_shape=(pltpu.VMEM((NY, NX, 32, CHIP), bf16), pltpu.VMEM((NY, NX, 4, CHIP), f32)),
        in_specs=[hbm] * 3,
        out_specs=(vmem, vmem),
        scratch_shapes=[
            pltpu.VMEM((4, FF), bf16),
            pltpu.VMEM((4, FF), bf16),
            pltpu.VMEM((4, WIDE), f32),
            pltpu.VMEM((64, 4, WIDE), bf16),
            pltpu.VMEM((63, 4, WIDE), bf16),
            pltpu.VMEM((4, 256), bf16),
            pltpu.VMEM((4, 128), bf16),
            pltpu.VMEM((NZ, 4, 256), bf16),
            pltpu.VMEM((NZ, NY, 4, 128), bf16),
            pltpu.VMEM((NZ, NX, 4, 128), bf16),
            dma((3,)),
            dma((13,)),
            dma((2,)), dma, dma((2,)), dma, dma, dma, dma, dma((2,)), dma, dma((3,)),
            dma((2, 5)), dma((2, 5)), dma((5,)), dma((4, 5)), dma((3,)), dma((4,)),
        ],
        compiler_params=pltpu.CompilerParams(collective_id=0, has_side_effects=True, vmem_limit_bytes=32 * 2**20),
        cost_estimate=pl.CostEstimate(flops=4 * FF * 8, bytes_accessed=32 * FF * 4, transcendentals=0),
    )(*(pltpu.with_memory_space_constraint(a, pltpu.HBM) for a in (base_weight, local_weight, momentum)))
    return pl.pallas_call(
        flush_kernel,
        out_shape=(pltpu.HBM((32, FF), bf16), pltpu.HBM((4, FF), f32)),
        in_specs=[vmem, vmem],
        out_specs=(hbm, hbm),
        scratch_shapes=[dma((2, NY, NX))],
        cost_estimate=pl.CostEstimate(flops=0, bytes_accessed=32 * FF * 4, transcendentals=0),
    )(*(pltpu.with_memory_space_constraint(a, pltpu.VMEM) for a in (gath, gath_m)))


def solution(mesh):
    return jax.shard_map(
        shards,
        mesh=mesh,
        in_specs=(P("fsdp", None), P("rep", "fsdp", None), P("fsdp", None)),
        out_specs=(P(), P("fsdp", None)),
        check_vma=False,
    )
```

time: 47.4 us -> 46.5 us (0.981)
  Pallas kernels: 46.6 us -> 45.6 us
    pallas_call x1, Pallas kernels: 45.1 us -> 43.7 us  [shards(): pl.pallas_call(kernel, out_shape=(pltpu.VMEM((NY, NX, 32, CHIP), bf16), p...]
where the time goes in v3:
time: 46.5 us; the launch traced here: 46.2 us
  Pallas kernels  45.6 us (98%)
  between operations  0.64 us (1%)
    pallas_call x1, Pallas kernels, shards(): pl.pallas_call(kernel, out_shape=(pltpu.VMEM((NY, NX, 32, CHIP), bf16), p...  43.7 us
    pallas_call x1, Pallas kernels, shards(): pl.pallas_call(flush_kernel, out_shape=(pltpu.HBM((32, FF), bf16), pltpu....  1.92 us

profile of v3, /device:TPU:1, one launch (start us, length us, event | category | flops | bytes accessed | tf_op | source)
XLA Modules:
  0.0 46.2 jit_solution(10539685181191283551)
XLA Ops:
  0.6 43.7 %shard_map.50 = (bf16[8,4,32,896]{3,2,1,0:T(8,128)(2,1)S(1)}, f32[8,4,4,896]{3,2,1,0:T(4,128)S(1)}) custom-call(bf16[4,28672]{1,0:T(4,128)(2,1)} %base_h.1, bf16[1,4,28672]{2,1,0:T(4,128)(2,1)} %local_h.1, f32[4,28672]{1,0:T(4,128)} %mom_h.1), custom_call_target="tpu_custom_call" | custom-call | flops 917504 | bytes 3670016 | tf_op jit(solution)/shard_map/pallas_call | solution.py:245
  44.3 1.9 %shard_map.51 = (bf16[32,28672]{1,0:T(8,128)(2,1)}, f32[4,28672]{1,0:T(4,128)}) custom-call(bf16[8,4,32,896]{3,2,1,0:T(8,128)(2,1)S(1)} %get-tuple-element.4.gath, f32[8,4,4,896]{3,2,1,0:T(4,128)S(1)} %get-tuple-element.5.gath_m), custom_call_target="tpu_custom_call" | custom-call | bytes 3670016 | tf_op jit(solution)/shard_map/pallas_call | solution.py:269

commit v4 on v3

--- a/solution.py
+++ b/solution.py
@@ -11,8 +11,8 @@
 CHIP = BLOCK // NX
 WIDE, NARROW = 512, 384
 SLOTS = (0, 1, -1, 2, -2, 3, -3, 4)
-GROUPS = ((0, 0, 1), (0, 1, 4), (0, 5, 3), (1, 0, 4), (1, 4, 4))
-DIRECT = (3, 4)
+GROUPS = ((0, 1), (1, 2), (3, 2), (5, 3))
+DIRECT = (3,)
 PLANE = sorted(((i, j, k) for i in range(NX) for j in range(NY) for k in range(2)),
                key=lambda d: (-min(d[0], NX - d[0]) - min(d[1], NY - d[1]), -d[2]))
 f32, bf16 = jnp.float32, jnp.bfloat16
@@ -29,9 +29,10 @@
 
 
 def kernel(base_h, local_h, mom_h, gath, gath_m, base_v, local_v, mom_v, send1, recv1, own_a, own_c, abuf, bbuf,
-           cbuf, in_sem, send_sem, r1, rz_a, ry_a, ry_b, rz_b, rx_c, rz_c, ry_c, ry_m, rx_m, rx, rh, rf, rc, rc_c, rc_m):
+           cbuf, in_sem, send_sem, r1, rz_a, ry_a, ry_b, rx_b, rz_b, rx_c, rz_c, ry_c, ry_m, rx_m, rx, rh, rf, rc, rc_b, rc_c,
+           rc_m):
     x, y, c, z = place()
-    s1, sz_a, sy_a, sy_b, sz_b, sx_c, sz_c, sy_c, sy_m, sx_m, sx, sc, sc_m = (send_sem.at[i] for i in range(13))
+    s1, sz_a, sy_a, sy_b, sx_b, sz_b, sx_c, sz_c, sy_c, sy_m, sx_m, sx, sc, sc_m = (send_sem.at[i] for i in range(14))
 
     def at(x_, y_, c_, z_):
         return {"rep": (x_ * NY + y_) * 2 + c_, "fsdp": z_}
@@ -94,13 +95,13 @@
     own_a[...] = new_b[:, :256]
     own_c[...] = new_b[:, 384:]
     abuf[z] = new_b[:, :256]
-    bbuf[z, 0] = new_b[:, 256:384]
+    bbuf[z, x, 0] = new_b[:, 256:384]
     cbuf[z, x] = new_b[:, 384:]
     for k in (2, 1, 3):
         remote(own_c, cbuf.at[z, x], sx_c, rx_c, x_peer(k))
     for k in SLOTS[:0:-1]:
         remote(own_a, abuf.at[z], sz_a, rz_a, z_peer(k))
-        remote(bbuf.at[z, 0], bbuf.at[z, slot_of(-k)], sy_b, ry_b, y_peer(k))
+        remote(bbuf.at[z, x, 0], bbuf.at[z, x, slot_of(-k)], sy_b, ry_b, y_peer(k))
 
     def rows(parts):
         return jnp.concatenate([p.astype(f32) for p in parts], axis=0).astype(bf16)
@@ -113,12 +114,10 @@
         cols = (pl.ds(par * WIDE, w_a), pl.ds(par * WIDE + w_a, 128), pl.ds(par * WIDE + w_a + 128, 128))
 
         def blocks(i, x_):
-            part_, start, n = GROUPS[i]
-            return gath.at[pl.ds(start, n), x_, :, cols[part_]]
+            return gath.at[pl.ds(*GROUPS[i]), x_, :, cols[0]]
 
         def halves(i, d, x_):
-            part_, start, n = GROUPS[i]
-            return gath.at[pl.ds(start, n), x_, pl.ds(d * 16, 16), cols[part_]]
+            return gath.at[pl.ds(*GROUPS[i]), x_, pl.ds(d * 16, 16), cols[0]]
 
         def pass_on(i, x_, k):
             remote(blocks(i, x_), blocks(i, x_), sc, rc.at[k, i], partner)
@@ -155,63 +154,72 @@
         drain(cbuf.at[0, pl.ds(0, 3)], rx_c)
         for k in SLOTS[:0:-1]:
             remote(cbuf.at[z], cbuf.at[z], sz_c, rz_c, z_peer(k))
+        drain(bbuf.at[0, 0, pl.ds(0, 7)], ry_b)
+        for k in (2, 1, 3):
+            remote(bbuf.at[z, x], bbuf.at[z, x], sx_b, rx_b, x_peer(k))
         drain(abuf.at[pl.ds(0, 7)], rz_a)
         gath[0, x, :, cols[0]] = rows([abuf[i][:, lo:] for i in range(NZ)])
         for k in SLOTS[1:]:
             slot = slot_of(-k)
-            remote(gath.at[0, x, :, cols[0]], gath.at[slot, x, :, cols[0]], sy_a, ry_a.at[int(slot > 4)], y_peer(k))
-        drain(bbuf.at[0, pl.ds(0, 7)], ry_b)
-        for k in SLOTS[:0:-1]:
-            remote(bbuf.at[z], bbuf.at[z], sz_b, rz_b, z_peer(k))
+            group = max(i for i in range(len(GROUPS)) if GROUPS[i][0] <= slot)
+            remote(gath.at[0, x, :, cols[0]], gath.at[slot, x, :, cols[0]], sy_a, ry_a.at[group - 1], y_peer(k))
         feed(0)
         drain(gath_m.at[pl.ds(0, 7), 0, :, own], ry_m)
         for k in (2, 1, 3):
             remote(momentum(x), momentum(x), sx_m, rx_m.at[k - 1], x_peer(k))
         remote(momentum(x), momentum(x), sc_m, rc_m.at[0], partner)
+        drain(bbuf.at[0, pl.ds(0, 3)], rx_b)
+        for k in SLOTS[:0:-1]:
+            remote(bbuf.at[z], bbuf.at[z], sz_b, rz_b, z_peer(k))
         drain(cbuf.at[pl.ds(0, 7)], rz_c)
         for i in range(NX):
             gath[0, i, :, cols[2]] = rows([cbuf[j, i] for j in range(NZ)])
         for k in SLOTS[:0:-1]:
             slot = slot_of(-k)
             remote(gath.at[0, :, :, cols[2]], gath.at[slot, :, :, cols[2]], sy_c, ry_c.at[int(slot > 4)], y_peer(k))
-        remote(gath.at[0, :, :, cols[2]], gath.at[0, :, :, cols[2]], sc, rc_c.at[0], partner)
-        drain(blocks(1, 0), ry_a.at[0])
-        feed(1)
-        take(0)
-        drain(blocks(2, 0), ry_a.at[1])
-        feed(2)
-        drain(bbuf.at[pl.ds(0, 7)], rz_b)
-        for s in range(NY):
-            gath[s, x, :, cols[1]] = rows([bbuf[i, s] for i in range(NZ)])
-            if s == 3:
-                feed(3)
-        feed(4)
-        take(1)
+
+        def pass_all(slots, part_, recv):
+            block = gath.at[pl.ds(*slots), :, :, cols[part_]]
+            remote(block, block, sc, recv, partner)
+
+        def pass_c(i, slots):
+            drain(gath.at[pl.ds(*slots), :, :, cols[2]], ry_c.at[i])
+            pass_all(slots, 2, rc_c.at[1 + i])
+
+        pass_all((0, 1), 2, rc_c.at[0])
+        for i in range(1, len(GROUPS)):
+            drain(blocks(i, 0), ry_a.at[i - 1])
+            feed(i)
+            take(i - 1)
         for k in (1, 3, 2):
             drain(momentum(0), rx_m.at[k - 1])
             remote(momentum((x - k) % NX), momentum((x - k) % NX), sc_m, rc_m.at[k], partner)
-        far(0)
-        take(2)
-        take(3)
-        take(4)
-        for i, near in ((1, pl.ds(1, 4)), (2, pl.ds(5, 3))):
+        for i in range(len(GROUPS) - 2):
             far(i)
-            block = gath.at[near, :, :, cols[2]]
-            drain(block, ry_c.at[i - 1])
-            remote(block, block, sc, rc_c.at[i], partner)
-        far(3)
-        far(4)
+        take(len(GROUPS) - 1)
+        pass_c(0, (1, 4))
+        far(len(GROUPS) - 2)
+        drain(bbuf.at[pl.ds(0, 7)], rz_b)
+        for s in range(NY):
+            for i in range(NX):
+                gath[s, i, :, cols[1]] = rows([bbuf[j, i, s] for j in range(NZ)])
+            if s % 4 == 3:
+                pass_all((s - 3, 4), 1, rc_b.at[s // 4])
+        pass_c(1, (5, 3))
+        far(len(GROUPS) - 1)
         drain(gath_m.at[pl.ds(0, 7), 0, :, own], sy_m)
         drain(gath.at[pl.ds(0, 7), 0, :, cols[0]], sy_a)
         drain(gath.at[pl.ds(0, 7), :, :, cols[2]], sy_c)
         drain(gath_m.at[:, pl.ds(0, 3), :, own], sx_m)
         drain(gath_m.at[:, :, :, own], sc_m)
-        drain(gath.at[:, pl.ds(0, 3), :, pl.ds(0, w_a + 128)], sx)
+        drain(gath.at[:, pl.ds(0, 3), :, cols[0]], sx)
         drain(gath.at[:, :, :, own], sc)
         for k in range(4):
             drain(gath_m.at[:, 0, :, pl.ds(0, other)], rc_m.at[k])
-            for i, (part_, start, n) in enumerate(GROUPS):
-                drain(gath.at[pl.ds(start, n), 0, :, pl.ds(0, 128 if part_ else other - 256)], rc.at[k, i])
+            for i, group in enumerate(GROUPS):
+                drain(gath.at[pl.ds(*group), 0, :, pl.ds(0, other - 256)], rc.at[k, i])
+        for i in range(2):
+            drain(gath.at[pl.ds(0, 4), :, :, pl.ds(0, 128)], rc_b.at[i])
         for i, n in enumerate((1, 4, 3)):
             drain(gath.at[pl.ds(0, n), :, :, pl.ds(0, 128)], rc_c.at[i])
 
@@ -219,7 +227,8 @@
         pl.when(c == par)(lambda par=par: gather(par))
     drain(recv1, s1)
     drain(abuf.at[pl.ds(0, 7)], sz_a)
-    drain(bbuf.at[0, pl.ds(0, 7)], sy_b)
+    drain(bbuf.at[0, 0, pl.ds(0, 7)], sy_b)
+    drain(bbuf.at[0, pl.ds(0, 3)], sx_b)
     drain(bbuf.at[pl.ds(0, 7)], sz_b)
     drain(cbuf.at[0, pl.ds(0, 3)], sx_c)
     drain(cbuf.at[pl.ds(0, 7)], sz_c)
@@ -241,7 +250,7 @@
 
 def shards(base_weight, local_weight, momentum):
     hbm, vmem = pl.BlockSpec(memory_space=pltpu.HBM), pl.BlockSpec(memory_space=pltpu.VMEM)
-    dma = pltpu.SemaphoreType.DMA
+    dma, n = pltpu.SemaphoreType.DMA, len(GROUPS)
     gath, gath_m = pl.pallas_call(
         kernel,
         out_shape=(pltpu.VMEM((NY, NX, 32, CHIP), bf16), pltpu.VMEM((NY, NX, 4, CHIP), f32)),
@@ -256,12 +265,12 @@
             pltpu.VMEM((4, 256), bf16),
             pltpu.VMEM((4, 128), bf16),
             pltpu.VMEM((NZ, 4, 256), bf16),
-            pltpu.VMEM((NZ, NY, 4, 128), bf16),
+            pltpu.VMEM((NZ, NX, NY, 4, 128), bf16),
             pltpu.VMEM((NZ, NX, 4, 128), bf16),
             dma((3,)),
-            dma((13,)),
-            dma((2,)), dma, dma((2,)), dma, dma, dma, dma, dma((2,)), dma, dma((3,)),
-            dma((2, 5)), dma((2, 5)), dma((5,)), dma((4, 5)), dma((3,)), dma((4,)),
+            dma((14,)),
+            dma((2,)), dma, dma((n,)), dma, dma, dma, dma, dma, dma((2,)), dma, dma((3,)),
+            dma((2, n)), dma((2, n)), dma((n,)), dma((4, n)), dma((2,)), dma((3,)), dma((4,)),
         ],
         compiler_params=pltpu.CompilerParams(collective_id=0, has_side_effects=True, vmem_limit_bytes=32 * 2**20),
         cost_estimate=pl.CostEstimate(flops=4 * FF * 8, bytes_accessed=32 * FF * 4, transcendentals=0),

time: 46.5 us -> 45.6 us (0.981)
  Pallas kernels: 45.6 us -> 44.8 us
    pallas_call x1, Pallas kernels: 43.7 us -> 42.9 us  [shards(): pl.pallas_call(kernel, out_shape=(pltpu.VMEM((NY, NX, 32, CHIP), bf16), p...]
where the time goes in v4:
time: 45.6 us; the launch traced here: 45.4 us
  Pallas kernels  44.8 us (98%)
  between operations  0.64 us (1%)
    pallas_call x1, Pallas kernels, shards(): pl.pallas_call(kernel, out_shape=(pltpu.VMEM((NY, NX, 32, CHIP), bf16), p...  42.9 us
    pallas_call x1, Pallas kernels, shards(): pl.pallas_call(flush_kernel, out_shape=(pltpu.HBM((32, FF), bf16), pltpu....  1.92 us

profile of v4, /device:TPU:1, one launch (start us, length us, event | category | flops | bytes accessed | tf_op | source)
XLA Modules:
  0.0 45.4 jit_solution(3413997051310411406)
XLA Ops:
  0.6 42.9 %shard_map.50 = (bf16[8,4,32,896]{3,2,1,0:T(8,128)(2,1)S(1)}, f32[8,4,4,896]{3,2,1,0:T(4,128)S(1)}) custom-call(bf16[4,28672]{1,0:T(4,128)(2,1)} %base_h.1, bf16[1,4,28672]{2,1,0:T(4,128)(2,1)} %local_h.1, f32[4,28672]{1,0:T(4,128)} %mom_h.1), custom_call_target="tpu_custom_call" | custom-call | flops 917504 | bytes 3670016 | tf_op jit(solution)/shard_map/pallas_call | solution.py:254
  43.5 1.9 %shard_map.51 = (bf16[32,28672]{1,0:T(8,128)(2,1)}, f32[4,28672]{1,0:T(4,128)}) custom-call(bf16[8,4,32,896]{3,2,1,0:T(8,128)(2,1)S(1)} %get-tuple-element.4.gath, f32[8,4,4,896]{3,2,1,0:T(4,128)S(1)} %get-tuple-element.5.gath_m), custom_call_target="tpu_custom_call" | custom-call | bytes 3670016 | tf_op jit(solution)/shard_map/pallas_call | solution.py:278

commit v5 on v4

v5 whole, which is shorter than its diff:
```python
import jax
import jax.numpy as jnp
from jax import lax
from jax.experimental import pallas as pl
from jax.experimental.pallas import tpu as pltpu
from jax.sharding import PartitionSpec as P

FF = 28672
NX, NY, NZ = 4, 8, 8
BLOCK = FF // NY
CHIP = BLOCK // NX
WIDE, NARROW = 512, 384
SLOTS = (0, 1, -1, 2, -2, 3, -3, 4)
GROUPS = ((0, 1), (1, 2), (3, 2), (5, 3))
DIRECT = (3,)
PLANE = sorted(((i, j, k) for i in range(NX) for j in range(NY) for k in range(2)),
               key=lambda d: (-min(d[0], NX - d[0]) - min(d[1], NY - d[1]), -d[2]))
f32, bf16 = jnp.float32, jnp.bfloat16
MESH = pl.DeviceIdType.MESH


def slot_of(offset):
    return SLOTS.index((offset + 3) % NY - 3)


def place():
    rep = lax.axis_index("rep")
    return rep // (2 * NY), (rep // 2) % NY, rep % 2, lax.axis_index("fsdp")


def kernel(base_h, local_h, mom_h, gath, gath_m, base_v, local_v, mom_v, send1, recv1, own_a, own_c, abuf, bbuf,
           cbuf, in_sem, send_sem, r1, rz_a, ry_a, ry_b, rx_b, rz_b, rx_c, rz_c, ry_c, ry_m, rx_m, rx, rh, rf, rc, rc_m):
    x, y, c, z = place()
    s1, s1_other, sz_a, sy_a, sy_b, sx_b, sz_b, sx_c, sz_c, sy_c, sy_m, sx_m, sx, sc, sc_m = (send_sem.at[i] for i in range(15))

    def at(x_, y_, c_, z_):
        return {"rep": (x_ * NY + y_) * 2 + c_, "fsdp": z_}

    def y_peer(k):
        return at(x, (y + k) % NY, c, z)

    def z_peer(k):
        return at(x, y, c, (z + k) % NZ)

    def x_peer(k):
        return at((x + k) % NX, y, c, z)

    partner = at(x, y, 1 - c, z)
    barrier = pltpu.get_barrier_semaphore()
    for dx, dy, dc in PLANE[:-1]:
        dev = at((x + dx) % NX, (y + dy) % NY, (c + dc) % 2, z)
        pl.semaphore_signal(barrier, inc=1, device_id=dev, device_id_type=MESH)
    for k in range(1, NZ):
        pl.semaphore_signal(barrier, inc=1, device_id=z_peer(k), device_id_type=MESH)

    def remote(src, dst, send, recv, dev):
        pltpu.make_async_remote_copy(src_ref=src, dst_ref=dst, send_sem=send, recv_sem=recv, device_id=dev,
                                     device_id_type=MESH).start()

    def drain(ref, sem):
        pltpu.make_async_copy(ref, ref, sem).wait()

    in_local = pltpu.make_async_copy(local_h.at[0], local_v, in_sem.at[0])
    in_base = pltpu.make_async_copy(base_h, base_v, in_sem.at[1])
    in_local.start()
    in_base.start()

    def rows(parts):
        return jnp.concatenate([p.astype(f32) for p in parts], axis=0).astype(bf16)

    def replicas(par):
        w, other = (WIDE, NARROW) if par == 0 else (NARROW, WIDE)
        w_a = w - 256
        own = pl.ds(par * WIDE, w)
        parts = (pl.ds(0, w_a), pl.ds(w_a, 128), pl.ds(w_a + 128, 128))
        cols = (pl.ds(par * WIDE, w_a), pl.ds(par * WIDE + w_a, 128), pl.ds(par * WIDE + w_a + 128, 128))

        def window(j, x_, core):
            return pl.ds(pl.multiple_of(j * BLOCK + x_ * CHIP + core * WIDE, 128), NARROW if core else WIDE)

        mine = window(y, x, par)
        in_mom = pltpu.make_async_copy(mom_h.at[:, mine], mom_v.at[:, pl.ds(0, w)], in_sem.at[2])
        in_mom.start()
        in_local.wait()
        in_base.wait()

        for k, (dx, dy, dc) in enumerate(PLANE):
            j, h, core = (y + dy) % NY, (x + dx) % NX, (par + dc) % 2
            there = window(j, h, core)
            part = pl.ds(0, there.size)
            send1[k, :, part] = (base_v[:, there].astype(f32) - local_v[:, there].astype(f32)).astype(bf16)
            if k == 0:
                pl.semaphore_wait(barrier, len(PLANE) - 1 + NZ - 1)
            if k < 63:
                remote(send1.at[k, :, part], recv1.at[k, :, part], s1_other if dc else s1, r1.at[k // 32], at(h, j, core, z))
        total = send1[63, :, pl.ds(0, w)].astype(f32)
        in_mom.wait()
        b = base_v[:, mine].astype(f32)
        for some in (range(32), range(32, 63)):
            drain(recv1.at[pl.ds(0, len(some)), :, pl.ds(0, w)], r1.at[some[0] // 32])
            for k in some:
                total += recv1[k, :, pl.ds(0, w)].astype(f32)
        grad = total * (1.0 / 64.0)
        new_m = 0.9 * mom_v[:, pl.ds(0, w)] + grad
        new_b = (b - 0.7 * (grad + 0.9 * new_m)).astype(bf16)
        own_a[:, parts[0]] = new_b[:, :w_a]
        abuf[z, :, parts[0]] = new_b[:, :w_a]
        bbuf[z, x, 0] = new_b[:, w_a:w_a + 128]
        own_c[...] = new_b[:, w_a + 128:]
        cbuf[z, x] = new_b[:, w_a + 128:]
        for k in (2, 1, 3):
            remote(own_c, cbuf.at[z, x], sx_c, rx_c, x_peer(k))
        for k in SLOTS[:0:-1]:
            remote(own_a.at[:, parts[0]], abuf.at[z, :, parts[0]], sz_a, rz_a, z_peer(k))
        for dx in (2, 1, 3, 0):
            for dy in SLOTS[::-1]:
                if dx or dy:
                    send, recv = (sx_b, rx_b) if dx else (sy_b, ry_b)
                    remote(bbuf.at[z, x, 0], bbuf.at[z, x, slot_of(-dy)], send, recv, at((x + dx) % NX, (y + dy) % NY, c, z))

        def blocks(i, x_):
            return gath.at[pl.ds(*GROUPS[i]), x_, :, cols[0]]

        def halves(i, d, x_):
            return gath.at[pl.ds(*GROUPS[i]), x_, pl.ds(d * 16, 16), cols[0]]

        def pass_on(i, x_):
            remote(blocks(i, x_), blocks(i, x_), sc, rc, partner)

        def feed(i):
            if i in DIRECT:
                remote(blocks(i, x), blocks(i, x), sx, rf.at[i], x_peer(2))
            for d, k in enumerate((1, -1)):
                remote(blocks(i, x), blocks(i, x), sx, rx.at[d, i], x_peer(k))
            pass_on(i, x)

        def take(i):
            for d, k in enumerate((1, -1)):
                from_ = (x - k) % NX
                drain(blocks(i, 0), rx.at[d, i])
                if i not in DIRECT:
                    remote(halves(i, d, from_), halves(i, d, from_), sx, rh.at[d, i], x_peer(k))
                pass_on(i, from_)

        def far(i):
            if i in DIRECT:
                drain(blocks(i, 0), rf.at[i])
            else:
                for d in range(2):
                    drain(halves(i, d, 0), rh.at[d, i])
            pass_on(i, (x + 2) % NX)

        def momentum(x_):
            return gath_m.at[:, x_, :, own]

        gath_m[0, x, :, own] = new_m
        for k in SLOTS[:0:-1]:
            remote(gath_m.at[0, x, :, own], gath_m.at[slot_of(-k), x, :, own], sy_m, ry_m, y_peer(k))
        drain(cbuf.at[0, pl.ds(0, 3)], rx_c)
        for k in SLOTS[:0:-1]:
            remote(cbuf.at[z], cbuf.at[z], sz_c, rz_c, z_peer(k))
        drain(abuf.at[pl.ds(0, 7), :, parts[0]], rz_a)
        gath[0, x, :, cols[0]] = rows([abuf[i, :, parts[0]] for i in range(NZ)])
        for k in SLOTS[1:]:
            slot = slot_of(-k)
            group = max(i for i in range(len(GROUPS)) if GROUPS[i][0] <= slot)
            remote(gath.at[0, x, :, cols[0]], gath.at[slot, x, :, cols[0]], sy_a, ry_a.at[group - 1], y_peer(k))
        feed(0)
        drain(bbuf.at[0, 0, pl.ds(0, 7)], ry_b)
        drain(bbuf.at[0, pl.ds(0, 3)], rx_b)
        for k in SLOTS[:0:-1]:
            remote(bbuf.at[z], bbuf.at[z], sz_b, rz_b, z_peer(k))
        drain(gath_m.at[pl.ds(0, 7), 0, :, own], ry_m)
        for k in (2, 1, 3):
            remote(momentum(x), momentum(x), sx_m, rx_m.at[k - 1], x_peer(k))
        remote(momentum(x), momentum(x), sc_m, rc_m, partner)
        drain(cbuf.at[pl.ds(0, 7)], rz_c)
        for i in range(NX):
            gath[0, i, :, cols[2]] = rows([cbuf[j, i] for j in range(NZ)])
        for k in SLOTS[:0:-1]:
            slot = slot_of(-k)
            remote(gath.at[0, :, :, cols[2]], gath.at[slot, :, :, cols[2]], sy_c, ry_c.at[int(slot > 4)], y_peer(k))

        def pass_all(slots, part_):
            block = gath.at[pl.ds(*slots), :, :, cols[part_]]
            remote(block, block, sc, rc, partner)

        def pass_c(i, slots):
            drain(gath.at[pl.ds(*slots), :, :, cols[2]], ry_c.at[i])
            pass_all(slots, 2)

        pass_all((0, 1), 2)
        for i in range(1, len(GROUPS)):
            drain(blocks(i, 0), ry_a.at[i - 1])
            feed(i)
            take(i - 1)
        for k in (1, 3, 2):
            drain(momentum(0), rx_m.at[k - 1])
            remote(momentum((x - k) % NX), momentum((x - k) % NX), sc_m, rc_m, partner)
        for i in range(len(GROUPS) - 2):
            far(i)
        take(len(GROUPS) - 1)
        pass_c(0, (1, 4))
        far(len(GROUPS) - 2)
        drain(gath_m.at[pl.ds(0, 7), 0, :, own], sy_m)
        drain(gath.at[pl.ds(0, 7), 0, :, cols[0]], sy_a)
        drain(gath_m.at[:, pl.ds(0, 3), :, own], sx_m)
        drain(recv1.at[pl.ds(0, 31), :, pl.ds(0, w)], s1)
        drain(recv1.at[pl.ds(0, 32), :, pl.ds(0, other)], s1_other)
        drain(abuf.at[pl.ds(0, 7), :, parts[0]], sz_a)
        drain(bbuf.at[0, 0, pl.ds(0, 7)], sy_b)
        drain(bbuf.at[0, pl.ds(0, 3)], sx_b)
        drain(cbuf.at[0, pl.ds(0, 3)], sx_c)
        drain(cbuf.at[pl.ds(0, 7)], sz_c)
        drain(bbuf.at[pl.ds(0, 7)], rz_b)
        for s in range(NY):
            for i in range(NX):
                gath[s, i, :, cols[1]] = rows([bbuf[j, i, s] for j in range(NZ)])
            if s % 2 == 1:
                pass_all((s - 1, 2), 1)
        pass_c(1, (5, 3))
        far(len(GROUPS) - 1)
        drain(gath.at[pl.ds(0, 7), :, :, cols[2]], sy_c)
        drain(gath.at[:, pl.ds(0, 3), :, cols[0]], sx)
        drain(bbuf.at[pl.ds(0, 7)], sz_b)
        drain(gath_m.at[:, :, :, own], sc_m)
        drain(gath.at[:, :, :, own], sc)
        theirs = pl.ds((1 - par) * WIDE, other)
        drain(gath_m.at[:, :, :, theirs], rc_m)
        drain(gath.at[:, :, :, theirs], rc)

    for par in range(2):
        pl.when(c == par)(lambda par=par: replicas(par))


def flush_kernel(gath, gath_m, newb, newm, sem):
    y = place()[1]
    for s, off in enumerate(SLOTS):
        for i in range(NX):
            cols = pl.ds(pl.multiple_of((y + off) % NY * BLOCK + i * CHIP, 128), CHIP)
            pltpu.make_async_copy(gath.at[s, i], newb.at[:, cols], sem.at[0]).start()
            pltpu.make_async_copy(gath_m.at[s, i], newm.at[:, cols], sem.at[1]).start()
    pltpu.make_async_copy(newb, newb, sem.at[0]).wait()
    pltpu.make_async_copy(newm, newm, sem.at[1]).wait()


def shards(base_weight, local_weight, momentum):
    hbm, vmem = pl.BlockSpec(memory_space=pltpu.HBM), pl.BlockSpec(memory_space=pltpu.VMEM)
    dma, n = pltpu.SemaphoreType.DMA, len(GROUPS)
    gath, gath_m = pl.pallas_call(
        kernel,
        out_shape=(pltpu.VMEM((NY, NX, 32, CHIP), bf16), pltpu.VMEM((NY, NX, 4, CHIP), f32)),
        in_specs=[hbm] * 3,
        out_specs=(vmem, vmem),
        scratch_shapes=[
            pltpu.VMEM((4, FF), bf16),
            pltpu.VMEM((4, FF), bf16),
            pltpu.VMEM((4, WIDE), f32),
            pltpu.VMEM((64, 4, WIDE), bf16),
            pltpu.VMEM((63, 4, WIDE), bf16),
            pltpu.VMEM((4, 256), bf16),
            pltpu.VMEM((4, 128), bf16),
            pltpu.VMEM((NZ, 4, 256), bf16),
            pltpu.VMEM((NZ, NX, NY, 4, 128), bf16),
            pltpu.VMEM((NZ, NX, 4, 128), bf16),
            dma((3,)),
            dma((15,)),
            dma((2,)), dma, dma((n,)), dma, dma, dma, dma, dma, dma((2,)), dma, dma((3,)),
            dma((2, n)), dma((2, n)), dma((n,)), dma, dma,
        ],
        compiler_params=pltpu.CompilerParams(collective_id=0, has_side_effects=True, vmem_limit_bytes=32 * 2**20),
        cost_estimate=pl.CostEstimate(flops=4 * FF * 8, bytes_accessed=32 * FF * 4, transcendentals=0),
    )(*(pltpu.with_memory_space_constraint(a, pltpu.HBM) for a in (base_weight, local_weight, momentum)))
    return pl.pallas_call(
        flush_kernel,
        out_shape=(pltpu.HBM((32, FF), bf16), pltpu.HBM((4, FF), f32)),
        in_specs=[vmem, vmem],
        out_specs=(hbm, hbm),
        scratch_shapes=[dma((2,))],
        cost_estimate=pl.CostEstimate(flops=0, bytes_accessed=32 * FF * 4, transcendentals=0),
    )(*(pltpu.with_memory_space_constraint(a, pltpu.VMEM) for a in (gath, gath_m)))


def solution(mesh):
    return jax.shard_map(
        shards,
        mesh=mesh,
        in_specs=(P("fsdp", None), P("rep", "fsdp", None), P("fsdp", None)),
        out_specs=(P(), P("fsdp", None)),
        check_vma=False,
    )
```

time: 45.6 us -> 44.1 us (0.967)
  Pallas kernels: 44.8 us -> 43.3 us
    pallas_call x1, Pallas kernels: 42.9 us -> 41.9 us  [shards(): pl.pallas_call(kernel, out_shape=(pltpu.VMEM((NY, NX, 32, CHIP), bf16), p...]
    pallas_call x1, Pallas kernels: 1.92 us -> 1.37 us  [shards(): pl.pallas_call(flush_kernel, out_shape=(pltpu.HBM((32, FF), bf16), pltpu....]
where the time goes in v5:
time: 44.1 us; the launch traced here: 43.9 us
  Pallas kernels  43.3 us (98%)
  between operations  0.64 us (1%)
    pallas_call x1, Pallas kernels, shards(): pl.pallas_call(kernel, out_shape=(pltpu.VMEM((NY, NX, 32, CHIP), bf16), p...  41.9 us
    pallas_call x1, Pallas kernels, shards(): pl.pallas_call(flush_kernel, out_shape=(pltpu.HBM((32, FF), bf16), pltpu....  1.37 us

profile of v5, /device:TPU:1, one launch (start us, length us, event | category | flops | bytes accessed | tf_op | source)
XLA Modules:
  0.0 43.9 jit_solution(1637274690319783387)
XLA Ops:
  0.6 41.9 %shard_map.50 = (bf16[8,4,32,896]{3,2,1,0:T(8,128)(2,1)S(1)}, f32[8,4,4,896]{3,2,1,0:T(4,128)S(1)}) custom-call(bf16[4,28672]{1,0:T(4,128)(2,1)} %base_h.1, bf16[1,4,28672]{2,1,0:T(4,128)(2,1)} %local_h.1, f32[4,28672]{1,0:T(4,128)} %mom_h.1), custom_call_target="tpu_custom_call" | custom-call | flops 917504 | bytes 3670016 | tf_op jit(solution)/shard_map/pallas_call | solution.py:250
  42.6 1.4 %shard_map.51 = (bf16[32,28672]{1,0:T(8,128)(2,1)}, f32[4,28672]{1,0:T(4,128)}) custom-call(bf16[8,4,32,896]{3,2,1,0:T(8,128)(2,1)S(1)} %get-tuple-element.4.gath, f32[8,4,4,896]{3,2,1,0:T(4,128)S(1)} %get-tuple-element.5.gath_m), custom_call_target="tpu_custom_call" | custom-call | bytes 3670016 | tf_op jit(solution)/shard_map/pallas_call | solution.py:274

commit v6 on v5

--- a/solution.py
+++ b/solution.py
@@ -11,8 +11,8 @@
 CHIP = BLOCK // NX
 WIDE, NARROW = 512, 384
 SLOTS = (0, 1, -1, 2, -2, 3, -3, 4)
-GROUPS = ((0, 1), (1, 2), (3, 2), (5, 3))
-DIRECT = (3,)
+GROUPS = ((0, 1), (1, 4), (5, 3))
+DIRECT = (1, 2)
 PLANE = sorted(((i, j, k) for i in range(NX) for j in range(NY) for k in range(2)),
                key=lambda d: (-min(d[0], NX - d[0]) - min(d[1], NY - d[1]), -d[2]))
 f32, bf16 = jnp.float32, jnp.bfloat16
@@ -108,10 +108,10 @@
         bbuf[z, x, 0] = new_b[:, w_a:w_a + 128]
         own_c[...] = new_b[:, w_a + 128:]
         cbuf[z, x] = new_b[:, w_a + 128:]
+        for k in SLOTS[:0:-1]:
+            remote(own_a.at[:, parts[0]], abuf.at[z, :, parts[0]], sz_a, rz_a, z_peer(k))
         for k in (2, 1, 3):
             remote(own_c, cbuf.at[z, x], sx_c, rx_c, x_peer(k))
-        for k in SLOTS[:0:-1]:
-            remote(own_a.at[:, parts[0]], abuf.at[z, :, parts[0]], sz_a, rz_a, z_peer(k))
         for dx in (2, 1, 3, 0):
             for dy in SLOTS[::-1]:
                 if dx or dy:
@@ -199,9 +199,6 @@
             remote(momentum((x - k) % NX), momentum((x - k) % NX), sc_m, rc_m, partner)
         for i in range(len(GROUPS) - 2):
             far(i)
-        take(len(GROUPS) - 1)
-        pass_c(0, (1, 4))
-        far(len(GROUPS) - 2)
         drain(gath_m.at[pl.ds(0, 7), 0, :, own], sy_m)
         drain(gath.at[pl.ds(0, 7), 0, :, cols[0]], sy_a)
         drain(gath_m.at[:, pl.ds(0, 3), :, own], sx_m)
@@ -218,6 +215,9 @@
                 gath[s, i, :, cols[1]] = rows([bbuf[j, i, s] for j in range(NZ)])
             if s % 2 == 1:
                 pass_all((s - 1, 2), 1)
+        take(len(GROUPS) - 1)
+        pass_c(0, (1, 4))
+        far(len(GROUPS) - 2)
         pass_c(1, (5, 3))
         far(len(GROUPS) - 1)
         drain(gath.at[pl.ds(0, 7), :, :, cols[2]], sy_c)

time: 44.1 us -> 43.9 us (level)
  no operation moved by 1% of the time
where the time goes in v6:
time: 43.9 us; the launch traced here: 43.8 us
  Pallas kernels  43.2 us (98%)
  between operations  0.64 us (1%)
    pallas_call x1, Pallas kernels, shards(): pl.pallas_call(kernel, out_shape=(pltpu.VMEM((NY, NX, 32, CHIP), bf16), p...  41.8 us
    pallas_call x1, Pallas kernels, shards(): pl.pallas_call(flush_kernel, out_shape=(pltpu.HBM((32, FF), bf16), pltpu....  1.37 us

profile of v6, /device:TPU:1, one launch (start us, length us, event | category | flops | bytes accessed | tf_op | source)
XLA Modules:
  0.0 43.8 jit_solution(12574819249909889704)
XLA Ops:
  0.6 41.8 %shard_map.50 = (bf16[8,4,32,896]{3,2,1,0:T(8,128)(2,1)S(1)}, f32[8,4,4,896]{3,2,1,0:T(4,128)S(1)}) custom-call(bf16[4,28672]{1,0:T(4,128)(2,1)} %base_h.1, bf16[1,4,28672]{2,1,0:T(4,128)(2,1)} %local_h.1, f32[4,28672]{1,0:T(4,128)} %mom_h.1), custom_call_target="tpu_custom_call" | custom-call | flops 917504 | bytes 3670016 | tf_op jit(solution)/shard_map/pallas_call | solution.py:250
  42.4 1.4 %shard_map.51 = (bf16[32,28672]{1,0:T(8,128)(2,1)}, f32[4,28672]{1,0:T(4,128)}) custom-call(bf16[8,4,32,896]{3,2,1,0:T(8,128)(2,1)S(1)} %get-tuple-element.4.gath, f32[8,4,4,896]{3,2,1,0:T(4,128)S(1)} %get-tuple-element.5.gath_m), custom_call_target="tpu_custom_call" | custom-call | bytes 3670016 | tf_op jit(solution)/shard_map/pallas_call | solution.py:274

commit v7 on v6

--- a/solution.py
+++ b/solution.py
@@ -12,7 +12,7 @@
 WIDE, NARROW = 512, 384
 SLOTS = (0, 1, -1, 2, -2, 3, -3, 4)
 GROUPS = ((0, 1), (1, 4), (5, 3))
-DIRECT = (1, 2)
+DIRECT = (0, 1, 2)
 PLANE = sorted(((i, j, k) for i in range(NX) for j in range(NY) for k in range(2)),
                key=lambda d: (-min(d[0], NX - d[0]) - min(d[1], NY - d[1]), -d[2]))
 f32, bf16 = jnp.float32, jnp.bfloat16

time: 43.9 us -> 43.9 us (level)
  no operation moved by 1% of the time
where the time goes in v7:
time: 43.9 us; the launch traced here: 43.7 us
  Pallas kernels  43.1 us (98%)
  between operations  0.64 us (1%)
    pallas_call x1, Pallas kernels, shards(): pl.pallas_call(kernel, out_shape=(pltpu.VMEM((NY, NX, 32, CHIP), bf16), p...  41.7 us
    pallas_call x1, Pallas kernels, shards(): pl.pallas_call(flush_kernel, out_shape=(pltpu.HBM((32, FF), bf16), pltpu....  1.37 us

profile of v7, /device:TPU:1, one launch (start us, length us, event | category | flops | bytes accessed | tf_op | source)
XLA Modules:
  0.0 43.7 jit_solution(13545249155817223474)
XLA Ops:
  0.6 41.7 %shard_map.50 = (bf16[8,4,32,896]{3,2,1,0:T(8,128)(2,1)S(1)}, f32[8,4,4,896]{3,2,1,0:T(4,128)S(1)}) custom-call(bf16[4,28672]{1,0:T(4,128)(2,1)} %base_h.1, bf16[1,4,28672]{2,1,0:T(4,128)(2,1)} %local_h.1, f32[4,28672]{1,0:T(4,128)} %mom_h.1), custom_call_target="tpu_custom_call" | custom-call | flops 917504 | bytes 3670016 | tf_op jit(solution)/shard_map/pallas_call | solution.py:250
  42.4 1.4 %shard_map.51 = (bf16[32,28672]{1,0:T(8,128)(2,1)}, f32[4,28672]{1,0:T(4,128)}) custom-call(bf16[8,4,32,896]{3,2,1,0:T(8,128)(2,1)S(1)} %get-tuple-element.4.gath, f32[8,4,4,896]{3,2,1,0:T(4,128)S(1)} %get-tuple-element.5.gath_m), custom_call_target="tpu_custom_call" | custom-call | bytes 3670016 | tf_op jit(solution)/shard_map/pallas_call | solution.py:274
